TPU v7x, 32 devices: a whole 2x2x4 slice. The times are simulated.
32 devices in a mesh: wide: 16 (over z, y, x), narrow: 2 (over core).
Axes of the slice: x: 2, y: 2, z: 4, core: 2. Of those that a mesh axis runs over, the one named last changes fastest.
Arguments:
- source: float32 [16, 256, 256], P('narrow', 'wide'), may hold values from -8 to 8
- start_pressure: float32 [16, 256, 256], P('narrow', 'wide'), may hold values from -4 to 4
- reaction: float32 [16, 256, 256], P('narrow', 'wide'), may hold values from 0.003 to 0.03
- couplings: float32 [6, 16, 256, 256], P(None, 'narrow', 'wide'), may hold values from 0.3 to 3
- run_lengths: int32 [2, 4], replicated, may hold values from 1 to 8, 16 in all within a row
Outputs:
- pressure: float32 [16, 256, 256], P('narrow', 'wide')
- coarse_correction: float32 [8, 128, 128], P('narrow', 'wide')
Inputs may be any that keep to these rules, and one draw needn't show every extreme that they name: `run_lengths`: each row lists, in order along the second dimension, the lengths of the runs of tile columns of that slab; a row sums to 16 and its largest entry is exactly 8.
All inputs are finite; a program needn't handle non-finite values.
Results may differ from a plain program's by a relative error of at most 0.00002.
Values sent between devices are 32-bit elements; how exact they have to be, the bound alone decides.
A program may use at most 64 MiB of HBM per device.

v0:
```python
import functools

import jax
import jax.numpy as jnp
from jax import lax
from jax.experimental import pallas as pl
from jax.experimental.pallas import tpu as pltpu
from jax.sharding import PartitionSpec as P

SWEEPS = 4
COARSE_SWEEPS = 4
STEPS = 2 * SWEEPS
MESH = pl.DeviceIdType.MESH
DOT = functools.partial(
    jnp.dot, precision=lax.Precision.HIGHEST, preferred_element_type=jnp.float32
)


def iota(shape, dim):
    return lax.broadcasted_iota(jnp.int32, shape, dim)


def kernel(
    n_wide,
    n_narrow,
    lengths_ref,
    source_ref,
    start_ref,
    reaction_ref,
    couplings_ref,
    pressure_ref,
    correction_ref,
    field,
    weights,
    scaled,
    diag,
    x_low,
    x_high,
    z_low,
    z_high,
    x_stage,
    z_stage,
    sums,
    operator,
    window,
    edge_low,
    edge_high,
    edge_stage,
    own_stage,
    spread,
    send_sem,
    recv_sem,
    op_send,
    op_recv,
    rhs_send,
    rhs_recv,
):
    depth, across, height = source_ref.shape
    cz, cx, cy = depth // 2, across // 2, height // 2
    wide = lax.axis_index("wide")
    narrow = lax.axis_index("narrow")
    there = {-1: wide > 0, 0: None, 1: wide < n_wide - 1}
    above = {-1: narrow > 0, 0: None, 1: narrow < n_narrow - 1}

    def exists(dx, dz):
        if dx == 0:
            return above[dz]
        if dz == 0:
            return there[dx]
        return jnp.logical_and(there[dx], above[dz])

    def target(dx, dz):
        return {"wide": wide + dx, "narrow": narrow + dz}

    around = [(dx, dz) for dx in (-1, 0, 1) for dz in (-1, 0, 1) if (dx, dz) != (0, 0)]

    for ref in (x_low, x_high, z_low, z_high, operator, window, edge_low, edge_high):
        ref[...] = jnp.zeros(ref.shape, ref.dtype)

    barrier = pltpu.get_barrier_semaphore()
    for dx, dz in around:

        @pl.when(exists(dx, dz))
        def _(dx=dx, dz=dz):
            pl.semaphore_signal(
                barrier, inc=1, device_id=target(dx, dz), device_id_type=MESH
            )

    beside = jnp.where(wide > 0, 1, 0) + jnp.where(wide < n_wide - 1, 1, 0)
    over = jnp.where(narrow > 0, 1, 0) + jnp.where(narrow < n_narrow - 1, 1, 0)
    pl.semaphore_wait(barrier, (beside + 1) * (over + 1) - 1)

    def faces(step):
        sides = [
            (-1, 0, x_stage.at[step, 0], x_high.at[step], 0),
            (1, 0, x_stage.at[step, 1], x_low.at[step], 1),
            (0, -1, z_stage.at[step, 0], z_high.at[step], 2),
            (0, 1, z_stage.at[step, 1], z_low.at[step], 3),
        ]
        return [
            (
                exists(dx, dz),
                pltpu.make_async_remote_copy(
                    src_ref=src,
                    dst_ref=dst,
                    send_sem=send_sem.at[step, which],
                    recv_sem=recv_sem.at[step, which],
                    device_id=target(dx, dz),
                    device_id_type=MESH,
                ),
            )
            for dx, dz, src, dst, which in sides
        ]

    def arrivals(step):
        order = [(1, 0, 0), (-1, 0, 1), (0, 1, 2), (0, -1, 3)]
        copies = faces(step)
        return [(exists(dx, dz), copies[which][1]) for dx, dz, which in order]

    def send(step, values):
        x_stage[step, 0] = values[:, 0:1, :]
        x_stage[step, 1] = values[:, across - 1 : across, :]
        z_stage[step, 0] = values[0]
        z_stage[step, 1] = values[depth - 1]
        for here, copy in faces(step):
            pl.when(here)(copy.start)

    send(0, start_ref[...])
    field[...] = start_ref[...]

    total = reaction_ref[...]
    for channel in range(6):
        total = total + couplings_ref[channel]
    diag[...] = total
    inverse = 1.0 / total
    scaled[...] = source_ref[...] * inverse
    lane = iota((depth, across, height), 2)
    for channel in range(6):
        scaled_weight = couplings_ref[channel] * inverse
        if channel == 4:
            scaled_weight = jnp.where(lane == 0, 0.0, scaled_weight)
        if channel == 5:
            scaled_weight = jnp.where(lane == height - 1, 0.0, scaled_weight)
        weights[channel] = scaled_weight

    fine_y = iota((height, cy), 0)
    coarse_y = iota((height, cy), 1)
    even = jnp.where(fine_y == 2 * coarse_y, 1.0, 0.0)
    odd = jnp.where(fine_y == 2 * coarse_y + 1, 1.0, 0.0)

    def in_z(take):
        low, high = [], []
        for z in range(cz):
            low.append(take(2 * z))
            high.append(take(2 * z + 1))
        return jnp.stack(low), jnp.stack(high)

    parts = []
    low, high = in_z(lambda z: reaction_ref[z])
    parts.append(low + high)
    parts.append(in_z(lambda z: couplings_ref[0, z])[0])
    parts.append(in_z(lambda z: couplings_ref[1, z])[1])
    for channel in (2, 3, 4, 5):
        low, high = in_z(lambda z: couplings_ref[channel, z])
        parts.append(low + high)
    for place, part in enumerate(parts):
        flat = part.reshape(cz * across, height)
        matrix = even if place == 5 else odd if place == 6 else even + odd
        sums[place] = DOT(flat, matrix).reshape(cz, across, cy)

    def pick(place, which):
        return sums[place, :, pl.ds(which, cx, stride=2), :]

    coarse = [pick(place, 0) + pick(place, 1) for place in (0, 1, 2)]
    coarse += [pick(3, 0), pick(4, 1)]
    coarse += [pick(place, 0) + pick(place, 1) for place in (5, 6)]
    coarse_diag = coarse[0]
    for channel in range(6):
        coarse_diag = coarse_diag + coarse[1 + channel]
    begin = jnp.int32(0)
    starts = jnp.int32(0)
    ends = jnp.int32(0)
    for run in range(lengths_ref.shape[1]):
        end = begin + lengths_ref[narrow, run]
        starts = starts + jnp.where(begin == wide, 1, 0)
        ends = ends + jnp.where(end - 1 == wide, 1, 0)
        begin = end
    block = (cz, cx, cy)
    at_z, at_x, at_y = iota(block, 0), iota(block, 1), iota(block, 2)
    cuts = [
        at_z == 0,
        at_z == cz - 1,
        jnp.where(at_x == 0, starts, 0) > 0,
        jnp.where(at_x == cx - 1, ends, 0) > 0,
        at_y == 0,
        at_y == cy - 1,
    ]
    coarse_inverse = 1.0 / coarse_diag
    for channel in range(6):
        operator[channel, :, cx : 2 * cx, :] = jnp.where(
            cuts[channel], 0.0, coarse[1 + channel] * coarse_inverse
        )
    operator[6, :, cx : 2 * cx, :] = coarse_inverse

    def operator_copy(dx, which):
        start = cx - cx * dx
        return pltpu.make_async_remote_copy(
            src_ref=operator.at[:, :, cx : 2 * cx, :],
            dst_ref=operator.at[:, :, start : start + cx, :],
            send_sem=op_send.at[which],
            recv_sem=op_recv.at[which],
            device_id=target(dx, 0),
            device_id_type=MESH,
        )

    for which, dx in enumerate((-1, 1)):
        pl.when(exists(dx, 0))(operator_copy(dx, which).start)

    row = iota((depth, across, height), 1)
    parity = (iota((depth, across, height), 0) + row + lane) % 2

    def relaxed(step):
        for here, copy in arrivals(step):
            pl.when(here)(copy.wait_recv)
        v = field[...]
        out = scaled[...]
        out = out + weights[0] * jnp.concatenate([z_low[step][None], v[:-1]], axis=0)
        out = out + weights[1] * jnp.concatenate([v[1:], z_high[step][None]], axis=0)
        west = jnp.where(row == 0, x_low[step], pltpu.roll(v, 1, 1))
        out = out + weights[2] * west
        east = jnp.where(row == across - 1, x_high[step], pltpu.roll(v, across - 1, 1))
        out = out + weights[3] * east
        out = out + weights[4] * pltpu.roll(v, 1, 2)
        out = out + weights[5] * pltpu.roll(v, height - 1, 2)
        return v, out

    def half_sweep(step, carry):
        v, out = relaxed(step)
        v = jnp.where(parity == step % 2, out, v)
        field[...] = v
        send(step + 1, v)
        return carry

    lax.fori_loop(0, STEPS, half_sweep, 0)
    v, out = relaxed(STEPS)
    residual = diag[...] * (out - v)

    offset = fine_y - 2 * coarse_y
    restrict = jnp.where(
        (offset == 0) | (offset == 1), 0.75, jnp.where((offset == -1) | (offset == 2), 0.25, 0.0)
    )
    along_y = DOT(residual.reshape(depth * across, height), restrict)
    along_y = along_y.reshape(depth, across, cy)
    edge_stage[0] = 0.25 * along_y[0]
    edge_stage[1] = 0.25 * along_y[depth - 1]
    base = 8
    own = base + across
    for z in range(cz):
        value = 0.75 * along_y[2 * z] + 0.75 * along_y[2 * z + 1]
        if z > 0:
            value = value + 0.25 * along_y[2 * z - 1]
        if z < cz - 1:
            value = value + 0.25 * along_y[2 * z + 2]
        window[z, own : own + across, :] = value
        own_stage[z] = value

    def window_copy(dx, dz, which):
        start = own - across * dx
        rows = slice(start, start + across)
        if dz == 0:
            src, dst = own_stage, window.at[:, rows, :]
        elif dz < 0:
            src, dst = edge_stage.at[0], edge_high.at[rows, :]
        else:
            src, dst = edge_stage.at[1], edge_low.at[rows, :]
        return pltpu.make_async_remote_copy(
            src_ref=src,
            dst_ref=dst,
            send_sem=rhs_send.at[which],
            recv_sem=rhs_recv.at[which],
            device_id=target(dx, dz),
            device_id_type=MESH,
        )

    for which, (dx, dz) in enumerate(around):
        pl.when(exists(dx, dz))(window_copy(dx, dz, which).start)
    for which, (dx, dz) in enumerate(around):
        pl.when(exists(-dx, -dz))(window_copy(dx, dz, which).wait_recv)
    for which, dx in enumerate((-1, 1)):
        pl.when(exists(-dx, 0))(operator_copy(dx, which).wait_recv)

    window[0] = window[0] + edge_low[...]
    window[cz - 1] = window[cz - 1] + edge_high[...]
    span = 3 * cx

    def take(offset):
        return window[:, pl.ds(base + offset, span, stride=2), :]

    rhs = 0.25 * take(-1) + 0.75 * take(0) + 0.75 * take(1) + 0.25 * take(2)
    rhs = rhs * operator[6]
    shape = (cz, span, cy)
    coarse_parity = (iota(shape, 0) + iota(shape, 1) + cx + iota(shape, 2)) % 2
    result = jnp.where(coarse_parity == 0, rhs, 0.0)
    for half in range(1, 2 * COARSE_SWEEPS):
        u = result
        out = rhs
        out = out + operator[0] * jnp.concatenate([u[-1:], u[:-1]], axis=0)
        out = out + operator[1] * jnp.concatenate([u[1:], u[:1]], axis=0)
        out = out + operator[2] * pltpu.roll(u, 1, 1)
        out = out + operator[3] * pltpu.roll(u, span - 1, 1)
        out = out + operator[4] * pltpu.roll(u, 1, 2)
        out = out + operator[5] * pltpu.roll(u, cy - 1, 2)
        result = jnp.where(coarse_parity == half % 2, out, u)

    correction = result[:, cx : 2 * cx, :]
    correction_ref[...] = correction
    flat = correction.reshape(cz * cx, cy)
    repeat = jnp.where(iota((cy, height), 0) == iota((cy, height), 1) // 2, 1.0, 0.0)
    wider = DOT(flat, repeat).reshape(cz, cx, height)
    for half in range(height // cy):
        piece = wider[:, :, half * cy : (half + 1) * cy]
        for which in range(2):
            spread[half, :, pl.ds(which, cx, stride=2), :] = piece
    for z in range(depth):
        for half in range(height // cy):
            lanes = slice(half * cy, (half + 1) * cy)
            pressure_ref[z, :, lanes] = field[z, :, lanes] + spread[half, z // 2]

    def drain(step, carry):
        for here, copy in faces(step):
            pl.when(here)(copy.wait_send)
        return carry

    lax.fori_loop(0, STEPS + 1, drain, 0)
    for which, dx in enumerate((-1, 1)):
        pl.when(exists(dx, 0))(operator_copy(dx, which).wait_send)
    for which, (dx, dz) in enumerate(around):
        pl.when(exists(dx, dz))(window_copy(dx, dz, which).wait_send)


def body(n_wide, n_narrow, source, start_pressure, reaction, couplings, run_lengths):
    depth, across, height = source.shape
    cz, cx, cy = depth // 2, across // 2, height // 2
    f32 = jnp.float32
    fine = (depth, across, height)
    rounds = STEPS + 1
    vmem = pl.BlockSpec(memory_space=pltpu.VMEM)
    return pl.pallas_call(
        functools.partial(kernel, n_wide, n_narrow),
        out_shape=(
            jax.ShapeDtypeStruct(fine, f32),
            jax.ShapeDtypeStruct((cz, cx, cy), f32),
        ),
        in_specs=[pl.BlockSpec(memory_space=pltpu.SMEM)] + [vmem] * 4,
        out_specs=(vmem, vmem),
        scratch_shapes=[
            pltpu.VMEM(fine, f32),
            pltpu.VMEM((6,) + fine, f32),
            pltpu.VMEM(fine, f32),
            pltpu.VMEM(fine, f32),
            pltpu.VMEM((rounds, depth, 1, height), f32),
            pltpu.VMEM((rounds, depth, 1, height), f32),
            pltpu.VMEM((rounds, across, height), f32),
            pltpu.VMEM((rounds, across, height), f32),
            pltpu.VMEM((rounds, 2, depth, 1, height), f32),
            pltpu.VMEM((rounds, 2, across, height), f32),
            pltpu.VMEM((7, cz, across, cy), f32),
            pltpu.VMEM((7, cz, 3 * cx, cy), f32),
            pltpu.VMEM((cz, 3 * across + 16, cy), f32),
            pltpu.VMEM((3 * across + 16, cy), f32),
            pltpu.VMEM((3 * across + 16, cy), f32),
            pltpu.VMEM((2, across, cy), f32),
            pltpu.VMEM((cz, across, cy), f32),
            pltpu.VMEM((2, cz, across, cy), f32),
            pltpu.SemaphoreType.DMA((rounds, 4)),
            pltpu.SemaphoreType.DMA((rounds, 4)),
            pltpu.SemaphoreType.DMA((2,)),
            pltpu.SemaphoreType.DMA((2,)),
            pltpu.SemaphoreType.DMA((8,)),
            pltpu.SemaphoreType.DMA((8,)),
        ],
        compiler_params=pltpu.CompilerParams(
            collective_id=0, has_side_effects=True, vmem_limit_bytes=32 * 1024 * 1024
        ),
    )(run_lengths, source, start_pressure, reaction, couplings)


def solution(mesh):
    placed = (
        P("narrow", "wide", None),
        P("narrow", "wide", None),
        P("narrow", "wide", None),
        P(None, "narrow", "wide", None),
        P(),
    )
    return jax.shard_map(
        functools.partial(body, mesh.shape["wide"], mesh.shape["narrow"]),
        mesh=mesh,
        in_specs=placed,
        out_specs=(P("narrow", "wide", None), P("narrow", "wide", None)),
        check_vma=False,
    )
```

profile of v0, /device:TPU:25, one launch (start us, length us, event | category | flops | bytes accessed | tf_op | source)
XLA Modules:
  0.0 49.2 jit_solution(9964839686922925693)
XLA Ops:
  0.6 0.0 copy-start
  0.6 1.1 %copy-done = f32[6,8,16,256]{3,2,1,0:T(8,128)S(1)} copy-done((f32[6,8,16,256]{3,2,1,0:T(8,128)S(1)}, f32[6,8,16,256]{3,2,1,0:T(8,128)}, u32[]{:S(2)}) %copy-start) | copy-done | bytes 786456
  1.8 0.0 copy-start.1
  1.8 0.9 %copy-done.1 = f32[8,16,256]{2,1,0:T(8,128)S(1)} copy-done((f32[8,16,256]{2,1,0:T(8,128)S(1)}, f32[8,16,256]{2,1,0:T(8,128)}, u32[]{:S(2)}) %copy-start.1) | copy-done | bytes 131096
  2.7 0.0 copy-start.2
  2.7 0.9 %copy-done.2 = f32[8,16,256]{2,1,0:T(8,128)S(1)} copy-done((f32[8,16,256]{2,1,0:T(8,128)S(1)}, f32[8,16,256]{2,1,0:T(8,128)}, u32[]{:S(2)}) %copy-start.2) | copy-done | bytes 131096
  3.6 0.0 copy-start.3
  3.6 0.9 %copy-done.3 = f32[8,16,256]{2,1,0:T(8,128)S(1)} copy-done((f32[8,16,256]{2,1,0:T(8,128)S(1)}, f32[8,16,256]{2,1,0:T(8,128)}, u32[]{:S(2)}) %copy-start.3) | copy-done | bytes 131096
  4.5 0.0 copy-start.4
  4.5 0.7 %copy-done.4 = s32[2,4]{1,0:T(2,128)S(1)} copy-done((s32[2,4]{1,0:T(2,128)S(1)}, s32[2,4]{1,0:T(2,128)}, u32[]{:S(2)}) %copy-start.4) | copy-done | bytes 56
  5.2 42.7 %shard_map.68 = (f32[8,16,256]{2,1,0:T(8,128)S(1)}, f32[4,8,128]{2,1,0:T(8,128)S(1)}) custom-call(s32[2,4]{1,0:T(2,128)S(1)} %copy-done.4, f32[8,16,256]{2,1,0:T(8,128)S(1)} %copy-done.1, f32[8,16,256]{2,1,0:T(8,128)S(1)} %copy-done.2, f32[8,16,256]{2,1,0:T(8,128)S(1)} %copy-done.3, f32[6,8,16,256]{3,2,1,0:T(8,128)S(1)} %copy-done), custom_call_target="tpu_custom_call" | custom-call | tf_op jit(solution)/shard_map/pallas_call | solution.py:348
  47.9 0.7 %copy.9 = f32[8,16,256]{2,1,0:T(8,128)} copy(f32[8,16,256]{2,1,0:T(8,128)S(1)} %get-tuple-element.4) | data formatting | bytes 262144
  48.6 0.6 %copy.10 = f32[4,8,128]{2,1,0:T(8,128)} copy(f32[4,8,128]{2,1,0:T(8,128)S(1)} %get-tuple-element.5) | data formatting | bytes 32768
Async XLA Ops:
  0.6 1.1 %copy-start = (f32[6,8,16,256]{3,2,1,0:T(8,128)S(1)}, f32[6,8,16,256]{3,2,1,0:T(8,128)}, u32[]{:S(2)}) copy-start(f32[6,8,16,256]{3,2,1,0:T(8,128)} %couplings_ref.1) | copy-start | bytes 2359300
  1.8 0.9 %copy-start.1 = (f32[8,16,256]{2,1,0:T(8,128)S(1)}, f32[8,16,256]{2,1,0:T(8,128)}, u32[]{:S(2)}) copy-start(f32[8,16,256]{2,1,0:T(8,128)} %source_ref.1) | copy-start | bytes 393220
  2.7 0.9 %copy-start.2 = (f32[8,16,256]{2,1,0:T(8,128)S(1)}, f32[8,16,256]{2,1,0:T(8,128)}, u32[]{:S(2)}) copy-start(f32[8,16,256]{2,1,0:T(8,128)} %start_ref.1) | copy-start | bytes 393220
  3.6 0.9 %copy-start.3 = (f32[8,16,256]{2,1,0:T(8,128)S(1)}, f32[8,16,256]{2,1,0:T(8,128)}, u32[]{:S(2)}) copy-start(f32[8,16,256]{2,1,0:T(8,128)} %reaction_ref.1) | copy-start | bytes 393220
  4.5 0.7 %copy-start.4 = (s32[2,4]{1,0:T(2,128)S(1)}, s32[2,4]{1,0:T(2,128)}, u32[]{:S(2)}) copy-start(s32[2,4]{1,0:T(2,128)} %lengths_ref.1) | copy-start | bytes 100
where the time goes:
time: 49.4 us; the launch traced here: 49.2 us
  Pallas kernels  42.7 us (86%)
  local copies, waits for them, and re-layouts  5.78 us (12%)
  between operations  0.65 us (1%)
    pallas_call x1, Pallas kernels, body(): pl.pallas_call(functools.partial(kernel, n_wide, n_narrow), out_shape=(ja...  42.7 us
    unnamed x12, local copies, waits for them, and re-layouts  5.78 us

commit v1 on v0

--- a/solution.py
+++ b/solution.py
@@ -10,6 +10,8 @@
 SWEEPS = 4
 COARSE_SWEEPS = 4
 STEPS = 2 * SWEEPS
+DEEP = 3
+ROUNDS = (STEPS + DEEP) // DEEP
 MESH = pl.DeviceIdType.MESH
 DOT = functools.partial(
     jnp.dot, precision=lax.Precision.HIGHEST, preferred_element_type=jnp.float32
@@ -24,21 +26,25 @@
     n_wide,
     n_narrow,
     lengths_ref,
+    source_hbm,
+    start_hbm,
+    reaction_hbm,
+    couplings_hbm,
+    pressure_ref,
+    correction_ref,
     source_ref,
-    start_ref,
     reaction_ref,
     couplings_ref,
-    pressure_ref,
-    correction_ref,
     field,
     weights,
-    scaled,
     diag,
-    x_low,
-    x_high,
+    halo,
+    x_stage,
+    border,
+    halo_weights,
+    weight_stage,
     z_low,
     z_high,
-    x_stage,
     z_stage,
     sums,
     operator,
@@ -48,14 +54,19 @@
     edge_stage,
     own_stage,
     spread,
-    send_sem,
-    recv_sem,
+    load_sem,
+    x_send,
+    x_recv,
+    z_send,
+    z_recv,
+    w_send,
+    w_recv,
     op_send,
     op_recv,
     rhs_send,
     rhs_recv,
 ):
-    depth, across, height = source_ref.shape
+    depth, across, height = field.shape
     cz, cx, cy = depth // 2, across // 2, height // 2
     wide = lax.axis_index("wide")
     narrow = lax.axis_index("narrow")
@@ -74,7 +85,21 @@
 
     around = [(dx, dz) for dx in (-1, 0, 1) for dz in (-1, 0, 1) if (dx, dz) != (0, 0)]
 
-    for ref in (x_low, x_high, z_low, z_high, operator, window, edge_low, edge_high):
+    loads = [
+        pltpu.make_async_copy(src, dst, load_sem.at[which])
+        for which, (src, dst) in enumerate(
+            (
+                (start_hbm, field),
+                (reaction_hbm, reaction_ref),
+                (couplings_hbm, couplings_ref),
+                (source_hbm, source_ref),
+            )
+        )
+    ]
+    for load in loads:
+        load.start()
+
+    for ref in (halo, halo_weights, z_low, z_high, operator, window, edge_low, edge_high):
         ref[...] = jnp.zeros(ref.shape, ref.dtype)
 
     barrier = pltpu.get_barrier_semaphore()
@@ -86,54 +111,63 @@
                 barrier, inc=1, device_id=target(dx, dz), device_id_type=MESH
             )
 
-    beside = jnp.where(wide > 0, 1, 0) + jnp.where(wide < n_wide - 1, 1, 0)
-    over = jnp.where(narrow > 0, 1, 0) + jnp.where(narrow < n_narrow - 1, 1, 0)
-    pl.semaphore_wait(barrier, (beside + 1) * (over + 1) - 1)
-
-    def faces(step):
-        sides = [
-            (-1, 0, x_stage.at[step, 0], x_high.at[step], 0),
-            (1, 0, x_stage.at[step, 1], x_low.at[step], 1),
-            (0, -1, z_stage.at[step, 0], z_high.at[step], 2),
-            (0, 1, z_stage.at[step, 1], z_low.at[step], 3),
-        ]
-        return [
-            (
-                exists(dx, dz),
-                pltpu.make_async_remote_copy(
-                    src_ref=src,
-                    dst_ref=dst,
-                    send_sem=send_sem.at[step, which],
-                    recv_sem=recv_sem.at[step, which],
-                    device_id=target(dx, dz),
-                    device_id_type=MESH,
-                ),
-            )
-            for dx, dz, src, dst, which in sides
-        ]
-
-    def arrivals(step):
-        order = [(1, 0, 0), (-1, 0, 1), (0, 1, 2), (0, -1, 3)]
-        copies = faces(step)
-        return [(exists(dx, dz), copies[which][1]) for dx, dz, which in order]
-
-    def send(step, values):
-        x_stage[step, 0] = values[:, 0:1, :]
-        x_stage[step, 1] = values[:, across - 1 : across, :]
-        z_stage[step, 0] = values[0]
-        z_stage[step, 1] = values[depth - 1]
-        for here, copy in faces(step):
-            pl.when(here)(copy.start)
-
-    send(0, start_ref[...])
-    field[...] = start_ref[...]
-
+    def remote(src, dst, send, recv, dx, dz):
+        return pltpu.make_async_remote_copy(
+            src_ref=src,
+            dst_ref=dst,
+            send_sem=send,
+            recv_sem=recv,
+            device_id=target(dx, dz),
+            device_id_type=MESH,
+        )
+
+    def x_copy(turn, side):
+        return remote(
+            x_stage.at[turn, side], halo.at[turn, 1 - side],
+            x_send.at[turn, side], x_recv.at[turn, side], 2 * side - 1, 0,
+        )
+
+    def weight_copy(side):
+        return remote(
+            weight_stage.at[side], halo_weights.at[1 - side],
+            w_send.at[side], w_recv.at[side], 2 * side - 1, 0,
+        )
+
+    def z_copy(step, side):
+        return remote(
+            z_stage.at[step, side], (z_low if side else z_high).at[step],
+            z_send.at[step, side], z_recv.at[step, side], 0, 2 * side - 1,
+        )
+
+    def start_x(copy):
+        for side in range(2):
+            pl.when(there[2 * side - 1])(copy(side).start)
+
+    def arrive_x(copy):
+        for side in range(2):
+            pl.when(there[1 - 2 * side])(copy(side).wait_recv)
+
+    def pack(store, layers):
+        for side in range(2):
+            for layer in range(layers):
+                at = across - 1 - layer if side else layer
+                for z in range(depth):
+                    store(side, layer, z, at)
+
+    def send_x(turn):
+        def store(side, layer, z, at):
+            x_stage[turn, side, layer, z : z + 1, :] = field[z, at : at + 1, :]
+
+        pack(store, DEEP)
+        start_x(functools.partial(x_copy, turn))
+
+    for load in loads:
+        load.wait()
     total = reaction_ref[...]
     for channel in range(6):
         total = total + couplings_ref[channel]
     diag[...] = total
     inverse = 1.0 / total
-    scaled[...] = source_ref[...] * inverse
     lane = iota((depth, across, height), 2)
     for channel in range(6):
         scaled_weight = couplings_ref[channel] * inverse
@@ -142,6 +176,19 @@
         if channel == 5:
             scaled_weight = jnp.where(lane == height - 1, 0.0, scaled_weight)
         weights[channel] = scaled_weight
+    weights[6] = source_ref[...] * inverse
+
+    def store_weights(side, layer, z, at):
+        for place in range(7):
+            weight_stage[side, layer, place, z : z + 1, :] = weights[place, z, at : at + 1, :]
+
+    pack(store_weights, DEEP - 1)
+
+    beside = jnp.where(wide > 0, 1, 0) + jnp.where(wide < n_wide - 1, 1, 0)
+    over = jnp.where(narrow > 0, 1, 0) + jnp.where(narrow < n_narrow - 1, 1, 0)
+    pl.semaphore_wait(barrier, (beside + 1) * (over + 1) - 1)
+    send_x(0)
+    start_x(weight_copy)
 
     fine_y = iota((height, cy), 0)
     coarse_y = iota((height, cy), 1)
@@ -202,48 +249,108 @@
         )
     operator[6, :, cx : 2 * cx, :] = coarse_inverse
 
-    def operator_copy(dx, which):
-        start = cx - cx * dx
-        return pltpu.make_async_remote_copy(
-            src_ref=operator.at[:, :, cx : 2 * cx, :],
-            dst_ref=operator.at[:, :, start : start + cx, :],
-            send_sem=op_send.at[which],
-            recv_sem=op_recv.at[which],
-            device_id=target(dx, 0),
-            device_id_type=MESH,
-        )
-
-    for which, dx in enumerate((-1, 1)):
-        pl.when(exists(dx, 0))(operator_copy(dx, which).start)
-
-    row = iota((depth, across, height), 1)
-    parity = (iota((depth, across, height), 0) + row + lane) % 2
-
-    def relaxed(step):
-        for here, copy in arrivals(step):
-            pl.when(here)(copy.wait_recv)
-        v = field[...]
-        out = scaled[...]
-        out = out + weights[0] * jnp.concatenate([z_low[step][None], v[:-1]], axis=0)
-        out = out + weights[1] * jnp.concatenate([v[1:], z_high[step][None]], axis=0)
-        west = jnp.where(row == 0, x_low[step], pltpu.roll(v, 1, 1))
-        out = out + weights[2] * west
-        east = jnp.where(row == across - 1, x_high[step], pltpu.roll(v, across - 1, 1))
-        out = out + weights[3] * east
-        out = out + weights[4] * pltpu.roll(v, 1, 2)
-        out = out + weights[5] * pltpu.roll(v, height - 1, 2)
+    def operator_copy(side):
+        start = 0 if side else 2 * cx
+        return remote(
+            operator.at[:, :, cx : 2 * cx, :], operator.at[:, :, start : start + cx, :],
+            op_send.at[side], op_recv.at[side], 2 * side - 1, 0,
+        )
+
+    row = iota((across, height), 0)
+    tile = row + iota((across, height), 1)
+    layer_row = iota((depth, height), 0)
+    layer_tile = layer_row + iota((depth, height), 1)
+    top = depth - 1
+
+    def exchange_z(step, turn):
+        for side, z in enumerate((0, top)):
+            z_stage[step, side, :across, :] = field[z]
+            for beside in range(2):
+                for layer in range(DEEP - 1):
+                    at = across + beside * (DEEP - 1) + layer
+                    z_stage[step, side, at : at + 1, :] = halo[turn, beside, layer, z : z + 1, :]
+        for side in range(2):
+            pl.when(above[2 * side - 1])(z_copy(step, side).start)
+        for side in range(2):
+            pl.when(above[1 - 2 * side])(z_copy(step, side).wait_recv)
+
+    def relaxed(z, step, sides):
+        v = field[z]
+        below = field[z - 1] if z > 0 else z_low[step, :across, :]
+        over = field[z + 1] if z < top else z_high[step, :across, :]
+        out = weights[6, z] + weights[0, z] * below + weights[1, z] * over
+        west = jnp.where(row == 0, sides[0][z : z + 1, :], pltpu.roll(v, 1, 0))
+        out = out + weights[2, z] * west
+        east = jnp.where(row == across - 1, sides[1][z : z + 1, :], pltpu.roll(v, across - 1, 0))
+        out = out + weights[3, z] * east
+        out = out + weights[4, z] * pltpu.roll(v, 1, 1)
+        out = out + weights[5, z] * pltpu.roll(v, height - 1, 1)
         return v, out
 
-    def half_sweep(step, carry):
-        v, out = relaxed(step)
-        v = jnp.where(parity == step % 2, out, v)
-        field[...] = v
-        send(step + 1, v)
+    def relax_layer(step, turn, side, layer, inner, outer):
+        h = halo[turn, side, layer]
+        w = halo_weights.at[side, layer]
+        at = across + side * (DEEP - 1) + layer
+        below = jnp.where(layer_row == 0, z_low[step, at : at + 1, :], pltpu.roll(h, 1, 0))
+        over = jnp.where(layer_row == top, z_high[step, at : at + 1, :], pltpu.roll(h, top, 0))
+        west, east = (inner, outer) if side else (outer, inner)
+        out = w[6] + w[0] * below + w[1] * over + w[2] * west + w[3] * east
+        out = out + w[4] * pltpu.roll(h, 1, 1) + w[5] * pltpu.roll(h, height - 1, 1)
+        colour = layer_tile + step + (layer if side else layer + 1)
+        halo[turn, side, layer] = jnp.where(colour % 2 == 0, out, h)
+
+    def pack_border(side, layer, z, at):
+        border[side, z : z + 1, :] = field[z, at : at + 1, :]
+
+    def half_sweep(turn, inside):
+        step = turn * DEEP + inside
+        exchange_z(step, turn)
+        colours = [(tile + step + z) % 2 == 0 for z in range(2)]
+        for z in range(depth):
+            v, out = relaxed(z, step, [halo.at[turn, side, 0] for side in range(2)])
+            field[z] = jnp.where(colours[z % 2], out, v)
+        if inside == 0:
+
+            @pl.when(turn == 0)
+            def _():
+                arrive_x(weight_copy)
+
+        for layer in range(DEEP - 1 - inside):
+            for side in range(2):
+                inner = border[side] if layer == 0 else halo[turn, side, layer - 1]
+                relax_layer(step, turn, side, layer, inner, halo[turn, side, layer + 1])
+        if inside < DEEP - 1:
+            pack(pack_border, 1)
+
+    def exchange_x(turn):
+        @pl.when(turn > 0)
+        def _():
+            send_x(turn)
+
+        @pl.when(turn == 1)
+        def _():
+            start_x(operator_copy)
+
+        pack(pack_border, 1)
+        arrive_x(functools.partial(x_copy, turn))
+
+    def full_round(turn, carry):
+        exchange_x(turn)
+        for inside in range(DEEP):
+            half_sweep(turn, inside)
         return carry
 
-    lax.fori_loop(0, STEPS, half_sweep, 0)
-    v, out = relaxed(STEPS)
-    residual = diag[...] * (out - v)
+    last = ROUNDS - 1
+    lax.fori_loop(0, last, full_round, 0)
+    exchange_x(last)
+    for inside in range(STEPS - last * DEEP):
+        half_sweep(last, inside)
+    exchange_z(STEPS, last)
+    residual = []
+    for z in range(depth):
+        v, out = relaxed(z, STEPS, [halo.at[last, side, 0] for side in range(2)])
+        residual.append(diag[z] * (out - v))
+    residual = jnp.stack(residual)
 
     offset = fine_y - 2 * coarse_y
     restrict = jnp.where(
@@ -286,8 +393,7 @@
         pl.when(exists(dx, dz))(window_copy(dx, dz, which).start)
     for which, (dx, dz) in enumerate(around):
         pl.when(exists(-dx, -dz))(window_copy(dx, dz, which).wait_recv)
-    for which, dx in enumerate((-1, 1)):
-        pl.when(exists(-dx, 0))(operator_copy(dx, which).wait_recv)
+    arrive_x(operator_copy)
 
     window[0] = window[0] + edge_low[...]
     window[cz - 1] = window[cz - 1] + edge_high[...]
@@ -326,14 +432,20 @@
             lanes = slice(half * cy, (half + 1) * cy)
             pressure_ref[z, :, lanes] = field[z, :, lanes] + spread[half, z // 2]
 
-    def drain(step, carry):
-        for here, copy in faces(step):
-            pl.when(here)(copy.wait_send)
+    def drain_z(step, carry):
+        for side in range(2):
+            pl.when(above[2 * side - 1])(z_copy(step, side).wait_send)
         return carry
 
-    lax.fori_loop(0, STEPS + 1, drain, 0)
-    for which, dx in enumerate((-1, 1)):
-        pl.when(exists(dx, 0))(operator_copy(dx, which).wait_send)
+    def drain_x(copy):
+        for side in range(2):
+            pl.when(there[2 * side - 1])(copy(side).wait_send)
+
+    lax.fori_loop(0, STEPS + 1, drain_z, 0)
+    for turn in range(ROUNDS):
+        drain_x(functools.partial(x_copy, turn))
+    drain_x(weight_copy)
+    drain_x(operator_copy)
     for which, (dx, dz) in enumerate(around):
         pl.when(exists(dx, dz))(window_copy(dx, dz, which).wait_send)
 
@@ -343,7 +455,11 @@
     cz, cx, cy = depth // 2, across // 2, height // 2
     f32 = jnp.float32
     fine = (depth, across, height)
-    rounds = STEPS + 1
+    steps = STEPS + 1
+    layers = DEEP - 1
+    face = across + 2 * layers
+    dma = pltpu.SemaphoreType.DMA
+    hbm = pl.BlockSpec(memory_space=pltpu.HBM)
     vmem = pl.BlockSpec(memory_space=pltpu.VMEM)
     return pl.pallas_call(
         functools.partial(kernel, n_wide, n_narrow),
@@ -351,19 +467,23 @@
             jax.ShapeDtypeStruct(fine, f32),
             jax.ShapeDtypeStruct((cz, cx, cy), f32),
         ),
-        in_specs=[pl.BlockSpec(memory_space=pltpu.SMEM)] + [vmem] * 4,
+        in_specs=[pl.BlockSpec(memory_space=pltpu.SMEM)] + [hbm] * 4,
         out_specs=(vmem, vmem),
         scratch_shapes=[
             pltpu.VMEM(fine, f32),
+            pltpu.VMEM(fine, f32),
             pltpu.VMEM((6,) + fine, f32),
             pltpu.VMEM(fine, f32),
+            pltpu.VMEM((7,) + fine, f32),
             pltpu.VMEM(fine, f32),
-            pltpu.VMEM((rounds, depth, 1, height), f32),
-            pltpu.VMEM((rounds, depth, 1, height), f32),
-            pltpu.VMEM((rounds, across, height), f32),
-            pltpu.VMEM((rounds, across, height), f32),
-            pltpu.VMEM((rounds, 2, depth, 1, height), f32),
-            pltpu.VMEM((rounds, 2, across, height), f32),
+            pltpu.VMEM((ROUNDS, 2, DEEP, depth, height), f32),
+            pltpu.VMEM((ROUNDS, 2, DEEP, depth, height), f32),
+            pltpu.VMEM((2, depth, height), f32),
+            pltpu.VMEM((2, layers, 7, depth, height), f32),
+            pltpu.VMEM((2, layers, 7, depth, height), f32),
+            pltpu.VMEM((steps, face, height), f32),
+            pltpu.VMEM((steps, face, height), f32),
+            pltpu.VMEM((steps, 2, face, height), f32),
             pltpu.VMEM((7, cz, across, cy), f32),
             pltpu.VMEM((7, cz, 3 * cx, cy), f32),
             pltpu.VMEM((cz, 3 * across + 16, cy), f32),
@@ -372,12 +492,17 @@
             pltpu.VMEM((2, across, cy), f32),
             pltpu.VMEM((cz, across, cy), f32),
             pltpu.VMEM((2, cz, across, cy), f32),
-            pltpu.SemaphoreType.DMA((rounds, 4)),
-            pltpu.SemaphoreType.DMA((rounds, 4)),
-            pltpu.SemaphoreType.DMA((2,)),
-            pltpu.SemaphoreType.DMA((2,)),
-            pltpu.SemaphoreType.DMA((8,)),
-            pltpu.SemaphoreType.DMA((8,)),
+            dma((4,)),
+            dma((ROUNDS, 2)),
+            dma((ROUNDS, 2)),
+            dma((steps, 2)),
+            dma((steps, 2)),
+            dma((2,)),
+            dma((2,)),
+            dma((2,)),
+            dma((2,)),
+            dma((8,)),
+            dma((8,)),
         ],
         compiler_params=pltpu.CompilerParams(
             collective_id=0, has_side_effects=True, vmem_limit_bytes=32 * 1024 * 1024

time: 49.4 us -> 40.9 us (0.83); the launches traced: 49.2 us -> 40.2 us
  Pallas kernels: 42.7 us -> 33.7 us
    pallas_call x1, Pallas kernels: 42.7 us -> 33.7 us  [body(): pl.pallas_call(functools.partial(kernel, n_wide, n_narrow), out_shape=(ja...]
where the time goes in v1:
time: 40.9 us; the launch traced here: 40.2 us
  Pallas kernels  33.7 us (82%)
  local copies, waits for them, and re-layouts  5.78 us (14%)
  between operations  0.65 us (2%)
    pallas_call x1, Pallas kernels, body(): pl.pallas_call(functools.partial(kernel, n_wide, n_narrow), out_shape=(ja...  33.7 us
    unnamed x12, local copies, waits for them, and re-layouts  5.78 us

profile of v1, /device:TPU:25, one launch (start us, length us, event | category | flops | bytes accessed | tf_op | source)
XLA Modules:
  0.0 40.2 jit_solution(1965035743113371474)
XLA Ops:
  0.6 0.0 copy-start
  0.6 1.1 %copy-done = f32[6,8,16,256]{3,2,1,0:T(8,128)S(1)} copy-done((f32[6,8,16,256]{3,2,1,0:T(8,128)S(1)}, f32[6,8,16,256]{3,2,1,0:T(8,128)}, u32[]{:S(2)}) %copy-start) | copy-done | bytes 786456
  1.8 0.0 copy-start.1
  1.8 0.9 %copy-done.1 = f32[8,16,256]{2,1,0:T(8,128)S(1)} copy-done((f32[8,16,256]{2,1,0:T(8,128)S(1)}, f32[8,16,256]{2,1,0:T(8,128)}, u32[]{:S(2)}) %copy-start.1) | copy-done | bytes 131096
  2.7 0.0 copy-start.2
  2.7 0.9 %copy-done.2 = f32[8,16,256]{2,1,0:T(8,128)S(1)} copy-done((f32[8,16,256]{2,1,0:T(8,128)S(1)}, f32[8,16,256]{2,1,0:T(8,128)}, u32[]{:S(2)}) %copy-start.2) | copy-done | bytes 131096
  3.6 0.0 copy-start.3
  3.6 0.9 %copy-done.3 = f32[8,16,256]{2,1,0:T(8,128)S(1)} copy-done((f32[8,16,256]{2,1,0:T(8,128)S(1)}, f32[8,16,256]{2,1,0:T(8,128)}, u32[]{:S(2)}) %copy-start.3) | copy-done | bytes 131096
  4.5 0.0 copy-start.4
  4.5 0.7 %copy-done.4 = s32[2,4]{1,0:T(2,128)S(1)} copy-done((s32[2,4]{1,0:T(2,128)S(1)}, s32[2,4]{1,0:T(2,128)}, u32[]{:S(2)}) %copy-start.4) | copy-done | bytes 56
  5.2 33.7 %shard_map.68 = (f32[8,16,256]{2,1,0:T(8,128)S(1)}, f32[4,8,128]{2,1,0:T(8,128)S(1)}) custom-call(s32[2,4]{1,0:T(2,128)S(1)} %copy-done.4, f32[8,16,256]{2,1,0:T(8,128)S(1)} %copy-done.1, f32[8,16,256]{2,1,0:T(8,128)S(1)} %copy-done.2, f32[8,16,256]{2,1,0:T(8,128)S(1)} %copy-done.3, f32[6,8,16,256]{3,2,1,0:T(8,128)S(1)} %copy-done), custom_call_target="tpu_custom_call" | custom-call | tf_op jit(solution)/shard_map/pallas_call | solution.py:464
  38.9 0.7 %copy.9 = f32[8,16,256]{2,1,0:T(8,128)} copy(f32[8,16,256]{2,1,0:T(8,128)S(1)} %get-tuple-element.4) | data formatting | bytes 262144
  39.6 0.6 %copy.10 = f32[4,8,128]{2,1,0:T(8,128)} copy(f32[4,8,128]{2,1,0:T(8,128)S(1)} %get-tuple-element.5) | data formatting | bytes 32768
Async XLA Ops:
  0.6 1.1 %copy-start = (f32[6,8,16,256]{3,2,1,0:T(8,128)S(1)}, f32[6,8,16,256]{3,2,1,0:T(8,128)}, u32[]{:S(2)}) copy-start(f32[6,8,16,256]{3,2,1,0:T(8,128)} %couplings_hbm.1) | copy-start | bytes 2359300
  1.8 0.9 %copy-start.1 = (f32[8,16,256]{2,1,0:T(8,128)S(1)}, f32[8,16,256]{2,1,0:T(8,128)}, u32[]{:S(2)}) copy-start(f32[8,16,256]{2,1,0:T(8,128)} %source_hbm.1) | copy-start | bytes 393220
  2.7 0.9 %copy-start.2 = (f32[8,16,256]{2,1,0:T(8,128)S(1)}, f32[8,16,256]{2,1,0:T(8,128)}, u32[]{:S(2)}) copy-start(f32[8,16,256]{2,1,0:T(8,128)} %start_hbm.1) | copy-start | bytes 393220
  3.6 0.9 %copy-start.3 = (f32[8,16,256]{2,1,0:T(8,128)S(1)}, f32[8,16,256]{2,1,0:T(8,128)}, u32[]{:S(2)}) copy-start(f32[8,16,256]{2,1,0:T(8,128)} %reaction_hbm.1) | copy-start | bytes 393220
  4.5 0.7 %copy-start.4 = (s32[2,4]{1,0:T(2,128)S(1)}, s32[2,4]{1,0:T(2,128)}, u32[]{:S(2)}) copy-start(s32[2,4]{1,0:T(2,128)} %lengths_ref.1) | copy-start | bytes 100

commit v2 on v1

--- a/solution.py
+++ b/solution.py
@@ -46,6 +46,9 @@
     z_low,
     z_high,
     z_stage,
+    layer_low,
+    layer_high,
+    layer_stage,
     sums,
     operator,
     window,
@@ -59,6 +62,8 @@
     x_recv,
     z_send,
     z_recv,
+    layer_send,
+    layer_recv,
     w_send,
     w_recv,
     op_send,
@@ -99,7 +104,7 @@
     for load in loads:
         load.start()
 
-    for ref in (halo, halo_weights, z_low, z_high, operator, window, edge_low, edge_high):
+    for ref in (halo, halo_weights, z_low, z_high, layer_low, layer_high, operator, window, edge_low, edge_high):
         ref[...] = jnp.zeros(ref.shape, ref.dtype)
 
     barrier = pltpu.get_barrier_semaphore()
@@ -139,6 +144,20 @@
             z_send.at[step, side], z_recv.at[step, side], 0, 2 * side - 1,
         )
 
+    def layer_copy(step, side):
+        return remote(
+            layer_stage.at[step, side], (layer_low if side else layer_high).at[step],
+            layer_send.at[step, side], layer_recv.at[step, side], 0, 2 * side - 1,
+        )
+
+    def start_z(copy):
+        for side in range(2):
+            pl.when(above[2 * side - 1])(copy(side).start)
+
+    def arrive_z(copy):
+        for side in range(2):
+            pl.when(above[1 - 2 * side])(copy(side).wait_recv)
+
     def start_x(copy):
         for side in range(2):
             pl.when(there[2 * side - 1])(copy(side).start)
@@ -160,6 +179,13 @@
 
         pack(store, DEEP)
         start_x(functools.partial(x_copy, turn))
+
+    top = depth - 1
+
+    def send_z(step):
+        for side, z in enumerate((0, top)):
+            z_stage[step, side] = field[z]
+        start_z(functools.partial(z_copy, step))
 
     for load in loads:
         load.wait()
@@ -189,6 +215,7 @@
     pl.semaphore_wait(barrier, (beside + 1) * (over + 1) - 1)
     send_x(0)
     start_x(weight_copy)
+    send_z(0)
 
     fine_y = iota((height, cy), 0)
     coarse_y = iota((height, cy), 1)
@@ -249,35 +276,31 @@
         )
     operator[6, :, cx : 2 * cx, :] = coarse_inverse
 
-    def operator_copy(side):
+    def operator_copy(channel, side):
         start = 0 if side else 2 * cx
         return remote(
-            operator.at[:, :, cx : 2 * cx, :], operator.at[:, :, start : start + cx, :],
-            op_send.at[side], op_recv.at[side], 2 * side - 1, 0,
+            operator.at[channel, :, cx : 2 * cx, :],
+            operator.at[channel, :, start : start + cx, :],
+            op_send.at[channel, side], op_recv.at[channel, side], 2 * side - 1, 0,
         )
 
     row = iota((across, height), 0)
     tile = row + iota((across, height), 1)
     layer_row = iota((depth, height), 0)
     layer_tile = layer_row + iota((depth, height), 1)
-    top = depth - 1
-
-    def exchange_z(step, turn):
+
+    def send_layers(step, turn):
         for side, z in enumerate((0, top)):
-            z_stage[step, side, :across, :] = field[z]
             for beside in range(2):
                 for layer in range(DEEP - 1):
-                    at = across + beside * (DEEP - 1) + layer
-                    z_stage[step, side, at : at + 1, :] = halo[turn, beside, layer, z : z + 1, :]
-        for side in range(2):
-            pl.when(above[2 * side - 1])(z_copy(step, side).start)
-        for side in range(2):
-            pl.when(above[1 - 2 * side])(z_copy(step, side).wait_recv)
+                    at = beside * (DEEP - 1) + layer
+                    layer_stage[step, side, at : at + 1, :] = halo[turn, beside, layer, z : z + 1, :]
+        start_z(functools.partial(layer_copy, step))
 
     def relaxed(z, step, sides):
         v = field[z]
-        below = field[z - 1] if z > 0 else z_low[step, :across, :]
-        over = field[z + 1] if z < top else z_high[step, :across, :]
+        below = field[z - 1] if z > 0 else z_low[step]
+        over = field[z + 1] if z < top else z_high[step]
         out = weights[6, z] + weights[0, z] * below + weights[1, z] * over
         west = jnp.where(row == 0, sides[0][z : z + 1, :], pltpu.roll(v, 1, 0))
         out = out + weights[2, z] * west
@@ -290,9 +313,9 @@
     def relax_layer(step, turn, side, layer, inner, outer):
         h = halo[turn, side, layer]
         w = halo_weights.at[side, layer]
-        at = across + side * (DEEP - 1) + layer
-        below = jnp.where(layer_row == 0, z_low[step, at : at + 1, :], pltpu.roll(h, 1, 0))
-        over = jnp.where(layer_row == top, z_high[step, at : at + 1, :], pltpu.roll(h, top, 0))
+        at = side * (DEEP - 1) + layer
+        below = jnp.where(layer_row == 0, layer_low[step, at : at + 1, :], pltpu.roll(h, 1, 0))
+        over = jnp.where(layer_row == top, layer_high[step, at : at + 1, :], pltpu.roll(h, top, 0))
         west, east = (inner, outer) if side else (outer, inner)
         out = w[6] + w[0] * below + w[1] * over + w[2] * west + w[3] * east
         out = out + w[4] * pltpu.roll(h, 1, 1) + w[5] * pltpu.roll(h, height - 1, 1)
@@ -302,37 +325,53 @@
     def pack_border(side, layer, z, at):
         border[side, z : z + 1, :] = field[z, at : at + 1, :]
 
+    inner_planes = list(range(1, top))
+
     def half_sweep(turn, inside):
         step = turn * DEEP + inside
-        exchange_z(step, turn)
         colours = [(tile + step + z) % 2 == 0 for z in range(2)]
-        for z in range(depth):
+
+        def update(z):
             v, out = relaxed(z, step, [halo.at[turn, side, 0] for side in range(2)])
             field[z] = jnp.where(colours[z % 2], out, v)
-        if inside == 0:
-
-            @pl.when(turn == 0)
-            def _():
-                arrive_x(weight_copy)
-
-        for layer in range(DEEP - 1 - inside):
-            for side in range(2):
-                inner = border[side] if layer == 0 else halo[turn, side, layer - 1]
-                relax_layer(step, turn, side, layer, inner, halo[turn, side, layer + 1])
+
+        arrive_z(functools.partial(z_copy, step))
+        update(0)
+        update(top)
+        send_z(step + 1)
+
+        @pl.when(step > 0)
+        def _():
+            start_x(functools.partial(operator_copy, step - 1))
+
+        for z in inner_planes:
+            update(z)
         if inside < DEEP - 1:
-            pack(pack_border, 1)
+            if inside == 0:
+
+                @pl.when(turn == 0)
+                def _():
+                    arrive_x(weight_copy)
+
+            arrive_z(functools.partial(layer_copy, step))
+            for layer in range(DEEP - 1 - inside):
+                for side in range(2):
+                    if layer > 0:
+                        inner = halo[turn, side, layer - 1]
+                    else:
+                        inner = border[side] if inside else x_stage[turn, side, 0]
+                    relax_layer(step, turn, side, layer, inner, halo[turn, side, layer + 1])
+            if inside + 1 < DEEP - 1:
+                send_layers(step + 1, turn)
+                pack(pack_border, 1)
 
     def exchange_x(turn):
         @pl.when(turn > 0)
         def _():
             send_x(turn)
 
-        @pl.when(turn == 1)
-        def _():
-            start_x(operator_copy)
-
-        pack(pack_border, 1)
         arrive_x(functools.partial(x_copy, turn))
+        send_layers(turn * DEEP, turn)
 
     def full_round(turn, carry):
         exchange_x(turn)
@@ -345,11 +384,17 @@
     exchange_x(last)
     for inside in range(STEPS - last * DEEP):
         half_sweep(last, inside)
-    exchange_z(STEPS, last)
-    residual = []
-    for z in range(depth):
+    residual = [None] * depth
+
+    def take_residual(z):
         v, out = relaxed(z, STEPS, [halo.at[last, side, 0] for side in range(2)])
-        residual.append(diag[z] * (out - v))
+        residual[z] = diag[z] * (out - v)
+
+    for z in inner_planes:
+        take_residual(z)
+    arrive_z(functools.partial(z_copy, STEPS))
+    take_residual(0)
+    take_residual(top)
     residual = jnp.stack(residual)
 
     offset = fine_y - 2 * coarse_y
@@ -393,7 +438,8 @@
         pl.when(exists(dx, dz))(window_copy(dx, dz, which).start)
     for which, (dx, dz) in enumerate(around):
         pl.when(exists(-dx, -dz))(window_copy(dx, dz, which).wait_recv)
-    arrive_x(operator_copy)
+    for channel in range(7):
+        arrive_x(functools.partial(operator_copy, channel))
 
     window[0] = window[0] + edge_low[...]
     window[cz - 1] = window[cz - 1] + edge_high[...]
@@ -432,20 +478,27 @@
             lanes = slice(half * cy, (half + 1) * cy)
             pressure_ref[z, :, lanes] = field[z, :, lanes] + spread[half, z // 2]
 
-    def drain_z(step, carry):
-        for side in range(2):
-            pl.when(above[2 * side - 1])(z_copy(step, side).wait_send)
-        return carry
+    def drain_z(copy):
+        def one(step, carry):
+            for side in range(2):
+                pl.when(above[2 * side - 1])(copy(step, side).wait_send)
+            return carry
+
+        return one
 
     def drain_x(copy):
         for side in range(2):
             pl.when(there[2 * side - 1])(copy(side).wait_send)
 
-    lax.fori_loop(0, STEPS + 1, drain_z, 0)
+    lax.fori_loop(0, STEPS + 1, drain_z(z_copy), 0)
+    for step in range(STEPS):
+        if step % DEEP < DEEP - 1:
+            drain_z(layer_copy)(step, 0)
     for turn in range(ROUNDS):
         drain_x(functools.partial(x_copy, turn))
     drain_x(weight_copy)
-    drain_x(operator_copy)
+    for channel in range(7):
+        drain_x(functools.partial(operator_copy, channel))
     for which, (dx, dz) in enumerate(around):
         pl.when(exists(dx, dz))(window_copy(dx, dz, which).wait_send)
 
@@ -457,7 +510,7 @@
     fine = (depth, across, height)
     steps = STEPS + 1
     layers = DEEP - 1
-    face = across + 2 * layers
+    face = 2 * layers
     dma = pltpu.SemaphoreType.DMA
     hbm = pl.BlockSpec(memory_space=pltpu.HBM)
     vmem = pl.BlockSpec(memory_space=pltpu.VMEM)
@@ -481,6 +534,9 @@
             pltpu.VMEM((2, depth, height), f32),
             pltpu.VMEM((2, layers, 7, depth, height), f32),
             pltpu.VMEM((2, layers, 7, depth, height), f32),
+            pltpu.VMEM((steps, across, height), f32),
+            pltpu.VMEM((steps, across, height), f32),
+            pltpu.VMEM((steps, 2, across, height), f32),
             pltpu.VMEM((steps, face, height), f32),
             pltpu.VMEM((steps, face, height), f32),
             pltpu.VMEM((steps, 2, face, height), f32),
@@ -497,10 +553,12 @@
             dma((ROUNDS, 2)),
             dma((steps, 2)),
             dma((steps, 2)),
+            dma((steps, 2)),
+            dma((steps, 2)),
             dma((2,)),
             dma((2,)),
-            dma((2,)),
-            dma((2,)),
+            dma((7, 2)),
+            dma((7, 2)),
             dma((8,)),
             dma((8,)),
         ],

time: 40.9 us -> 37.7 us (0.922)
  Pallas kernels: 33.7 us -> 30.8 us
    pallas_call x1, Pallas kernels: 33.7 us -> 30.8 us  [body(): pl.pallas_call(functools.partial(kernel, n_wide, n_narrow), out_shape=(ja...]
where the time goes in v2:
time: 37.7 us; the launch traced here: 37.2 us
  Pallas kernels  30.8 us (82%)
  local copies, waits for them, and re-layouts  5.78 us (15%)
  between operations  0.65 us (2%)
    pallas_call x1, Pallas kernels, body(): pl.pallas_call(functools.partial(kernel, n_wide, n_narrow), out_shape=(ja...  30.8 us
    unnamed x12, local copies, waits for them, and re-layouts  5.78 us

profile of v2, /device:TPU:25, one launch (start us, length us, event | category | flops | bytes accessed | tf_op | source)
XLA Modules:
  0.0 37.2 jit_solution(15878303911904235391)
XLA Ops:
  0.6 0.0 copy-start
  0.6 1.1 %copy-done = f32[6,8,16,256]{3,2,1,0:T(8,128)S(1)} copy-done((f32[6,8,16,256]{3,2,1,0:T(8,128)S(1)}, f32[6,8,16,256]{3,2,1,0:T(8,128)}, u32[]{:S(2)}) %copy-start) | copy-done | bytes 786456
  1.8 0.0 copy-start.1
  1.8 0.9 %copy-done.1 = f32[8,16,256]{2,1,0:T(8,128)S(1)} copy-done((f32[8,16,256]{2,1,0:T(8,128)S(1)}, f32[8,16,256]{2,1,0:T(8,128)}, u32[]{:S(2)}) %copy-start.1) | copy-done | bytes 131096
  2.7 0.0 copy-start.2
  2.7 0.9 %copy-done.2 = f32[8,16,256]{2,1,0:T(8,128)S(1)} copy-done((f32[8,16,256]{2,1,0:T(8,128)S(1)}, f32[8,16,256]{2,1,0:T(8,128)}, u32[]{:S(2)}) %copy-start.2) | copy-done | bytes 131096
  3.6 0.0 copy-start.3
  3.6 0.9 %copy-done.3 = f32[8,16,256]{2,1,0:T(8,128)S(1)} copy-done((f32[8,16,256]{2,1,0:T(8,128)S(1)}, f32[8,16,256]{2,1,0:T(8,128)}, u32[]{:S(2)}) %copy-start.3) | copy-done | bytes 131096
  4.5 0.0 copy-start.4
  4.5 0.7 %copy-done.4 = s32[2,4]{1,0:T(2,128)S(1)} copy-done((s32[2,4]{1,0:T(2,128)S(1)}, s32[2,4]{1,0:T(2,128)}, u32[]{:S(2)}) %copy-start.4) | copy-done | bytes 56
  5.2 30.8 %shard_map.68 = (f32[8,16,256]{2,1,0:T(8,128)S(1)}, f32[4,8,128]{2,1,0:T(8,128)S(1)}) custom-call(s32[2,4]{1,0:T(2,128)S(1)} %copy-done.4, f32[8,16,256]{2,1,0:T(8,128)S(1)} %copy-done.1, f32[8,16,256]{2,1,0:T(8,128)S(1)} %copy-done.2, f32[8,16,256]{2,1,0:T(8,128)S(1)} %copy-done.3, f32[6,8,16,256]{3,2,1,0:T(8,128)S(1)} %copy-done), custom_call_target="tpu_custom_call" | custom-call | tf_op jit(solution)/shard_map/pallas_call | solution.py:517
  36.0 0.7 %copy.9 = f32[8,16,256]{2,1,0:T(8,128)} copy(f32[8,16,256]{2,1,0:T(8,128)S(1)} %get-tuple-element.4) | data formatting | bytes 262144
  36.6 0.6 %copy.10 = f32[4,8,128]{2,1,0:T(8,128)} copy(f32[4,8,128]{2,1,0:T(8,128)S(1)} %get-tuple-element.5) | data formatting | bytes 32768
Async XLA Ops:
  0.6 1.1 %copy-start = (f32[6,8,16,256]{3,2,1,0:T(8,128)S(1)}, f32[6,8,16,256]{3,2,1,0:T(8,128)}, u32[]{:S(2)}) copy-start(f32[6,8,16,256]{3,2,1,0:T(8,128)} %couplings_hbm.1) | copy-start | bytes 2359300
  1.8 0.9 %copy-start.1 = (f32[8,16,256]{2,1,0:T(8,128)S(1)}, f32[8,16,256]{2,1,0:T(8,128)}, u32[]{:S(2)}) copy-start(f32[8,16,256]{2,1,0:T(8,128)} %source_hbm.1) | copy-start | bytes 393220
  2.7 0.9 %copy-start.2 = (f32[8,16,256]{2,1,0:T(8,128)S(1)}, f32[8,16,256]{2,1,0:T(8,128)}, u32[]{:S(2)}) copy-start(f32[8,16,256]{2,1,0:T(8,128)} %start_hbm.1) | copy-start | bytes 393220
  3.6 0.9 %copy-start.3 = (f32[8,16,256]{2,1,0:T(8,128)S(1)}, f32[8,16,256]{2,1,0:T(8,128)}, u32[]{:S(2)}) copy-start(f32[8,16,256]{2,1,0:T(8,128)} %reaction_hbm.1) | copy-start | bytes 393220
  4.5 0.7 %copy-start.4 = (s32[2,4]{1,0:T(2,128)S(1)}, s32[2,4]{1,0:T(2,128)}, u32[]{:S(2)}) copy-start(s32[2,4]{1,0:T(2,128)} %lengths_ref.1) | copy-start | bytes 100

commit v3 on v2

--- a/solution.py
+++ b/solution.py
@@ -132,10 +132,10 @@
             x_send.at[turn, side], x_recv.at[turn, side], 2 * side - 1, 0,
         )
 
-    def weight_copy(side):
+    def weight_copy(layer, side):
         return remote(
-            weight_stage.at[side], halo_weights.at[1 - side],
-            w_send.at[side], w_recv.at[side], 2 * side - 1, 0,
+            weight_stage.at[side, layer], halo_weights.at[1 - side, layer],
+            w_send.at[layer, side], w_recv.at[layer, side], 2 * side - 1, 0,
         )
 
     def z_copy(step, side):
@@ -214,7 +214,8 @@
     over = jnp.where(narrow > 0, 1, 0) + jnp.where(narrow < n_narrow - 1, 1, 0)
     pl.semaphore_wait(barrier, (beside + 1) * (over + 1) - 1)
     send_x(0)
-    start_x(weight_copy)
+    for layer in range(DEEP - 1):
+        start_x(functools.partial(weight_copy, layer))
     send_z(0)
 
     fine_y = iota((height, cy), 0)
@@ -347,20 +348,20 @@
         for z in inner_planes:
             update(z)
         if inside < DEEP - 1:
-            if inside == 0:
-
-                @pl.when(turn == 0)
-                def _():
-                    arrive_x(weight_copy)
+
+            @pl.when(turn == 0)
+            def _():
+                arrive_x(functools.partial(weight_copy, inside))
 
             arrive_z(functools.partial(layer_copy, step))
-            for layer in range(DEEP - 1 - inside):
+            for layer in range(inside, -1, -1):
                 for side in range(2):
                     if layer > 0:
                         inner = halo[turn, side, layer - 1]
                     else:
                         inner = border[side] if inside else x_stage[turn, side, 0]
-                    relax_layer(step, turn, side, layer, inner, halo[turn, side, layer + 1])
+                    outer = halo[turn, side, layer + 1]
+                    relax_layer(step - layer, turn, side, layer, inner, outer)
             if inside + 1 < DEEP - 1:
                 send_layers(step + 1, turn)
                 pack(pack_border, 1)
@@ -496,7 +497,8 @@
             drain_z(layer_copy)(step, 0)
     for turn in range(ROUNDS):
         drain_x(functools.partial(x_copy, turn))
-    drain_x(weight_copy)
+    for layer in range(DEEP - 1):
+        drain_x(functools.partial(weight_copy, layer))
     for channel in range(7):
         drain_x(functools.partial(operator_copy, channel))
     for which, (dx, dz) in enumerate(around):
@@ -555,8 +557,8 @@
             dma((steps, 2)),
             dma((steps, 2)),
             dma((steps, 2)),
-            dma((2,)),
-            dma((2,)),
+            dma((layers, 2)),
+            dma((layers, 2)),
             dma((7, 2)),
             dma((7, 2)),
             dma((8,)),

time: 37.7 us -> 37 us (0.981)
  Pallas kernels: 30.8 us -> 30 us
    pallas_call x1, Pallas kernels: 30.8 us -> 30 us  [body(): pl.pallas_call(functools.partial(kernel, n_wide, n_narrow), out_shape=(ja...]
where the time goes in v3:
time: 37 us; the launch traced here: 36.4 us
  Pallas kernels  30 us (81%)
  local copies, waits for them, and re-layouts  5.78 us (16%)
  between operations  0.65 us (2%)
    pallas_call x1, Pallas kernels, body(): pl.pallas_call(functools.partial(kernel, n_wide, n_narrow), out_shape=(ja...  30 us
    unnamed x12, local copies, waits for them, and re-layouts  5.78 us

profile of v3, /device:TPU:25, one launch (start us, length us, event | category | flops | bytes accessed | tf_op | source)
XLA Modules:
  0.0 36.4 jit_solution(17273058726814001893)
XLA Ops:
  0.6 0.0 copy-start
  0.6 1.1 %copy-done = f32[6,8,16,256]{3,2,1,0:T(8,128)S(1)} copy-done((f32[6,8,16,256]{3,2,1,0:T(8,128)S(1)}, f32[6,8,16,256]{3,2,1,0:T(8,128)}, u32[]{:S(2)}) %copy-start) | copy-done | bytes 786456
  1.8 0.0 copy-start.1
  1.8 0.9 %copy-done.1 = f32[8,16,256]{2,1,0:T(8,128)S(1)} copy-done((f32[8,16,256]{2,1,0:T(8,128)S(1)}, f32[8,16,256]{2,1,0:T(8,128)}, u32[]{:S(2)}) %copy-start.1) | copy-done | bytes 131096
  2.7 0.0 copy-start.2
  2.7 0.9 %copy-done.2 = f32[8,16,256]{2,1,0:T(8,128)S(1)} copy-done((f32[8,16,256]{2,1,0:T(8,128)S(1)}, f32[8,16,256]{2,1,0:T(8,128)}, u32[]{:S(2)}) %copy-start.2) | copy-done | bytes 131096
  3.6 0.0 copy-start.3
  3.6 0.9 %copy-done.3 = f32[8,16,256]{2,1,0:T(8,128)S(1)} copy-done((f32[8,16,256]{2,1,0:T(8,128)S(1)}, f32[8,16,256]{2,1,0:T(8,128)}, u32[]{:S(2)}) %copy-start.3) | copy-done | bytes 131096
  4.5 0.0 copy-start.4
  4.5 0.7 %copy-done.4 = s32[2,4]{1,0:T(2,128)S(1)} copy-done((s32[2,4]{1,0:T(2,128)S(1)}, s32[2,4]{1,0:T(2,128)}, u32[]{:S(2)}) %copy-start.4) | copy-done | bytes 56
  5.2 30.0 %shard_map.68 = (f32[8,16,256]{2,1,0:T(8,128)S(1)}, f32[4,8,128]{2,1,0:T(8,128)S(1)}) custom-call(s32[2,4]{1,0:T(2,128)S(1)} %copy-done.4, f32[8,16,256]{2,1,0:T(8,128)S(1)} %copy-done.1, f32[8,16,256]{2,1,0:T(8,128)S(1)} %copy-done.2, f32[8,16,256]{2,1,0:T(8,128)S(1)} %copy-done.3, f32[6,8,16,256]{3,2,1,0:T(8,128)S(1)} %copy-done), custom_call_target="tpu_custom_call" | custom-call | tf_op jit(solution)/shard_map/pallas_call | solution.py:519
  35.2 0.7 %copy.9 = f32[8,16,256]{2,1,0:T(8,128)} copy(f32[8,16,256]{2,1,0:T(8,128)S(1)} %get-tuple-element.4) | data formatting | bytes 262144
  35.8 0.6 %copy.10 = f32[4,8,128]{2,1,0:T(8,128)} copy(f32[4,8,128]{2,1,0:T(8,128)S(1)} %get-tuple-element.5) | data formatting | bytes 32768
Async XLA Ops:
  0.6 1.1 %copy-start = (f32[6,8,16,256]{3,2,1,0:T(8,128)S(1)}, f32[6,8,16,256]{3,2,1,0:T(8,128)}, u32[]{:S(2)}) copy-start(f32[6,8,16,256]{3,2,1,0:T(8,128)} %couplings_hbm.1) | copy-start | bytes 2359300
  1.8 0.9 %copy-start.1 = (f32[8,16,256]{2,1,0:T(8,128)S(1)}, f32[8,16,256]{2,1,0:T(8,128)}, u32[]{:S(2)}) copy-start(f32[8,16,256]{2,1,0:T(8,128)} %source_hbm.1) | copy-start | bytes 393220
  2.7 0.9 %copy-start.2 = (f32[8,16,256]{2,1,0:T(8,128)S(1)}, f32[8,16,256]{2,1,0:T(8,128)}, u32[]{:S(2)}) copy-start(f32[8,16,256]{2,1,0:T(8,128)} %start_hbm.1) | copy-start | bytes 393220
  3.6 0.9 %copy-start.3 = (f32[8,16,256]{2,1,0:T(8,128)S(1)}, f32[8,16,256]{2,1,0:T(8,128)}, u32[]{:S(2)}) copy-start(f32[8,16,256]{2,1,0:T(8,128)} %reaction_hbm.1) | copy-start | bytes 393220
  4.5 0.7 %copy-start.4 = (s32[2,4]{1,0:T(2,128)S(1)}, s32[2,4]{1,0:T(2,128)}, u32[]{:S(2)}) copy-start(s32[2,4]{1,0:T(2,128)} %lengths_ref.1) | copy-start | bytes 100
